TPU v7x, 32 devices: a whole 2x2x4 slice. The times are simulated.
32 devices in a mesh: mem: 4 (over y, x), reg: 8 (over z, core).
Axes of the slice: x: 2, y: 2, z: 4, core: 2. Of those that a mesh axis runs over, the one named last changes fastest.
Arguments:
- ensemble: float32 [256, 8192], P('mem', 'reg'), may hold values from -6 to 6
- obs_pert: float32 [256, 8192], P('mem', 'reg'), may hold values from -45 to 45
- innovation: float32 [8192], P('reg'), may hold values from -6 to 6
- block_list: int32 [32, 8], P(('reg', 'mem')), may hold values from 0 to 63, as said below
- loc_weights: float32 [32, 8, 128], P(('reg', 'mem')), may hold values from 0.05 to 1
Outputs:
- analysis: float32 [256, 8192], P('mem', 'reg')
Inputs may be any that keep to these rules, and one draw needn't show every extreme that they name: `block_list`: each patch lists 8 different blocks. The regions split the patches and the blocks each into equal runs in order; a patch lists only blocks of its own region and of the regions just before and after it, and always the first and the last block of its own region.
All inputs are finite; a program needn't handle non-finite values.
Results may differ from a plain program's by a relative error of at most 0.0003.
Values sent between devices are 32-bit elements; how exact they have to be, the bound alone decides.
A program may use at most 64 MiB of HBM per device.

v0:
```python
import jax
import jax.numpy as jnp
from jax import lax
from jax.sharding import PartitionSpec as P

NEWTON = 8


def extended(cells, sides, width):
    for axis, dim in sides:
        count = lax.axis_size(axis)
        ends = count - 1
        head = lax.slice_in_dim(cells, 0, width, axis=dim)
        tail = lax.slice_in_dim(cells, cells.shape[dim] - width, cells.shape[dim], axis=dim)
        cells = jnp.concatenate(
            [
                lax.ppermute(tail, axis, [(i, (i + 1) % count) for i in range(ends)]),
                cells,
                lax.ppermute(head, axis, [((i + 1) % count, i) for i in range(ends)]),
            ],
            axis=dim,
        )
    return cells


def batched(first, second, form):
    return jnp.einsum(
        form, first, second, precision=lax.Precision.HIGHEST, preferred_element_type=jnp.float32
    )


def analyse(columns, blocks, innov_blocks, weights):
    members = columns.shape[0]
    ens_mean = jnp.mean(columns, axis=0)
    anomalies = columns - ens_mean[None]
    weighted = blocks * weights[None]
    gram_matrix = batched(weighted, blocks, "kpo,jpo->pkj")
    drive = batched(weighted, innov_blocks, "kpo,po->pk")
    identity = jnp.eye(members, dtype=jnp.float32)
    system = identity[None] + gram_matrix / (members - 1.0)
    trace_sum = jnp.trace(system, axis1=1, axis2=2)
    iterate_y = system / trace_sum[:, None, None]
    iterate_z = identity[None]
    for repeat in range(NEWTON):
        factor = 1.5 * identity[None] - 0.5 * batched(iterate_z, iterate_y, "pij,pjk->pik")
        iterate_y, iterate_z = (
            batched(iterate_y, factor, "pij,pjk->pik"),
            batched(factor, iterate_z, "pij,pjk->pik"),
        )
    root = iterate_z / jnp.sqrt(trace_sum)[:, None, None]
    half_step = batched(root, drive, "pij,pj->pi")
    mean_weights = batched(root, half_step, "pij,pj->pi") / (members - 1.0)
    transform = root + mean_weights[:, :, None]
    return ens_mean[None] + batched(transform, anomalies, "pkj,kps->jps")


def on_device(ensemble, obs_pert, innovation, block_list, loc_weights):
    members = ensemble.shape[0] * lax.axis_size("mem")
    patches_here = block_list.shape[0]
    block_size = loc_weights.shape[2]
    own_obs = obs_pert.shape[1]
    own_blocks = own_obs // block_size
    innov_row = innovation.reshape(1, own_obs)
    whole = lax.all_gather(obs_pert, "mem", axis=0, tiled=True)
    edged, edged_innov = (
        extended(whole, (("reg", 1),), own_obs),
        extended(innov_row, (("reg", 1),), own_obs),
    )
    columns = lax.all_to_all(ensemble, "mem", split_axis=1, concat_axis=0, tiled=True)
    columns = columns.reshape(members, patches_here, columns.shape[1] // patches_here)
    offset = (lax.axis_index("reg") - 1) * own_blocks
    local_blocks = block_list - offset
    edged_blocks = edged.reshape(members, 3 * own_blocks, block_size)
    blocks = jnp.take(edged_blocks, local_blocks, axis=1).reshape(members, patches_here, -1)
    innov_table = edged_innov.reshape(3 * own_blocks, block_size)
    innov_blocks = jnp.take(innov_table, local_blocks, axis=0).reshape(patches_here, -1)
    weights = loc_weights.reshape(patches_here, -1)
    updated = analyse(columns, blocks, innov_blocks, weights).reshape(members, -1)
    return lax.all_to_all(updated, "mem", split_axis=0, concat_axis=1, tiled=True)


def solution(mesh):
    return jax.shard_map(
        on_device,
        mesh=mesh,
        in_specs=(
            P("mem", "reg"),
            P("mem", "reg"),
            P("reg"),
            P(("reg", "mem"), None),
            P(("reg", "mem"), None, None),
        ),
        out_specs=P("mem", "reg"),
        check_vma=False,
    )
```

profile of v0, /device:TPU:1, one launch (start us, length us, event | category | flops | bytes accessed | tf_op | source)
XLA Modules:
  0.0 99.2 jit_solution(1614838078132990451)
XLA Ops:
  6.5 0.0 copy-start.3
  6.5 0.0 all-gather.2.cloned.1.call-start
  6.5 0.7 all-gather.2.cloned.1.call-update
  7.3 4.6 %collective-permute-start.2 = (f32[1,1024]{1,0:T(1,128)}, f32[1,1024]{1,0:T(1,128)S(1)}, u32[]{:S(2)}, u32[]{:S(2)}) collective-permute-start(f32[1,1024]{1,0:T(1,128)} %bitcast.114), channel_id=1, source_target_pairs={{0,1},{1,2},{2,3},{3,4},{4,5},{5,6},{6,7},{8,9},{9,10},{10,11},{11... | collective-permute-start | bytes 12296 | tf_op jit(solution)/shard_map/ppermute | solution.py:17
  11.9 1.9 %collective-permute-start.3 = (f32[1,1024]{1,0:T(1,128)}, f32[1,1024]{1,0:T(1,128)S(1)}, u32[]{:S(2)}, u32[]{:S(2)}) collective-permute-start(f32[1,1024]{1,0:T(1,128)} %bitcast.115), channel_id=1, source_target_pairs={{1,0},{2,1},{3,2},{4,3},{5,4},{6,5},{7,6},{9,8},{10,9},{11,10},{12... | collective-permute-start | bytes 12296 | tf_op jit(solution)/shard_map/ppermute | solution.py:19
  13.8 1.7 %copy.25 = f32[8,4,8,256]{3,2,0,1:T(8,128)} copy(f32[8,4,8,256]{3,2,1,0:T(8,128)} %bitcast.108) | data formatting | bytes 524288 | tf_op jit(solution)/shard_map/all_to_all | solution.py:69
  15.5 3.4 %all-to-all-start = ((f32[64,4,256]{2,0,1:T(8,128)}), f32[64,4,256]{2,0,1:T(8,128)S(1)}, u32[]{:S(2)}, u32[]{:S(2)}) async-start(f32[64,4,256]{2,0,1:T(8,128)} %bitcast.99), calls=%async_computation | async-start | bytes 524288 | tf_op jit(solution)/shard_map/all_to_all | solution.py:69
  18.9 0.7 and_bitcast_fusion
  19.6 0.1 broadcast_bitcast_fusion
  19.6 20.2 %all-gather.2.cloned.1.call-done = f32[256,1024]{1,0:T(8,128)} async-done(((f32[64,1024]{1,0:T(8,128)}), f32[256,1024]{1,0:T(8,128)}) %all-gather.2.cloned.1.call-update) | async-done | bytes 1048592 | tf_op jit(solution)/shard_map/all_gather | solution.py:64
  39.8 1.6 %copy.15 = f32[256,1024]{0,1:T(8,128)S(1)} copy(f32[256,1024]{1,0:T(8,128)} %all-gather.2.cloned.1.call-done) | data formatting | bytes 2097152 | tf_op jit(solution)/shard_map/all_gather | solution.py:64
  41.4 0.0 copy-start
  41.4 3.7 %collective-permute-start = (f32[256,1024]{0,1:T(8,128)S(1)}, f32[256,1024]{0,1:T(8,128)S(1)}, u32[]{:S(2)}, u32[]{:S(2)}) collective-permute-start(f32[256,1024]{0,1:T(8,128)S(1)} %copy.15), channel_id=1, source_target_pairs={{0,1},{1,2},{2,3},{3,4},{4,5},{5,6},{6,7},{8,9},{9,10},{10,11},{11... | collective-permute-start | bytes 3145736 | tf_op jit(solution)/shard_map/ppermute | solution.py:17
  45.1 1.9 %collective-permute-start.1 = (f32[256,1024]{0,1:T(8,128)S(1)}, f32[256,1024]{0,1:T(8,128)}, u32[]{:S(2)}, u32[]{:S(2)}) collective-permute-start(f32[256,1024]{0,1:T(8,128)S(1)} %copy.15), channel_id=1, source_target_pairs={{1,0},{2,1},{3,2},{4,3},{5,4},{6,5},{7,6},{9,8},{10,9},{11,10},{12... | collective-permute-start | bytes 3145736 | tf_op jit(solution)/shard_map/ppermute | solution.py:19
  47.0 0.0 collective-permute-done.2
  47.0 0.0 collective-permute-done.3
  47.1 0.0 copy-done.3
  47.1 0.6 gather_fusion.1
  47.6 0.1 bitcast_select_fusion.1
  47.7 0.0 all-to-all-done
  47.8 9.0 %collective-permute-done = f32[256,1024]{0,1:T(8,128)S(1)} collective-permute-done((f32[256,1024]{0,1:T(8,128)S(1)}, f32[256,1024]{0,1:T(8,128)S(1)}, u32[]{:S(2)}, u32[]{:S(2)}) %collective-permute-start) | collective-permute-done | bytes 1048608 | tf_op jit(solution)/shard_map/ppermute | solution.py:17
  56.8 0.0 copy-done
  56.8 0.0 copy-start.1
  56.8 1.0 copy-done.1
  57.8 3.5 %collective-permute-done.1 = f32[256,1024]{0,1:T(8,128)} collective-permute-done((f32[256,1024]{0,1:T(8,128)S(1)}, f32[256,1024]{0,1:T(8,128)}, u32[]{:S(2)}, u32[]{:S(2)}) %collective-permute-start.1) | collective-permute-done | bytes 1048608 | tf_op jit(solution)/shard_map/ppermute | solution.py:19
  61.3 2.1 %pad_maximum_fusion = f32[256,3072]{0,1:T(8,128)S(1)} fusion(f32[256,1024]{0,1:T(8,128)} %collective-permute-done.1, f32[256,1024]{0,1:T(8,128)} %copy-done, f32[256,1024]{0,1:T(8,128)} %copy-done.1), kind=kLoop, calls=%fused_computation.2 | loop fusion | flops 1572864 | bytes 6291456 | tf_op jit(solution)/shard_map/concatenate | solution.py:15
  63.4 2.3 %copy.18 = f32[256,24,128]{2,0,1:T(8,128)} copy(f32[256,24,128]{0,2,1:T(8,128)S(1)} %bitcast.100) | data formatting | bytes 6291456 | tf_op jit(solution)/shard_map/reshape | solution.py:73
  65.7 2.5 %gather_fusion = f32[8,256,128]{2,1,0:T(8,128)S(1)} fusion(f32[256,24,128]{2,0,1:T(8,128)} %copy.18, s32[1024]{0:T(1024)S(1)} %pad_clamp_fusion), kind=kCustom, calls=%fused_computation | custom fusion | bytes 2097184 | tf_op jit(solution)/shard_map/jit(_take)/gather | solution.py:74
  68.2 0.0 copy-start.2
  68.2 0.1 bitcast_select_fusion
  68.4 0.3 copy.20
  68.7 0.3 copy.19
  69.1 0.0 copy-done.2
  69.1 2.7 %select_reduce_fusion = (f32[]{:T(128)}, f32[256,256]{1,0:T(8,128)S(1)}) fusion(f32[256,1024]{0,1:T(8,128)S(1)} %bitcast.104, f32[256,1,1,1,1,1,1024]{0,6,5,4,3,2,1:T(8,128)S(1)} %bitcast.101, f32[1024]{0:T(1024)S(1)} %bitcast.110, pred[1024]{0:T(1024)(128)(4,1)S(1)} %broadcast_bitcast_fusion), kind=kOutput, calls=%fused_computation.38 | convolution fusion | flops 806223872 | bytes 2364420 | tf_op jit(solution)/shard_map/kpo,jpo->pkj/dot_general | solution.py:27
  71.8 1.0 fusion.7
  72.8 1.0 %fusion.21 = f32[256,256]{1,0:T(8,128)S(1)} fusion(f32[256,256]{1,0:T(8,128)S(1)} %fusion.7, f32[256,256]{1,0:T(8,128)S(1)} %get-tuple-element.8, f32[]{:T(128)} %get-tuple-element.7), kind=kOutput, calls=%fused_computation.44 | convolution fusion | flops 201392128 | bytes 786436 | tf_op jit(solution)/shard_map/pij,pjk->pik/dot_general | solution.py:27
  73.8 0.3 fusion.19
  74.1 0.4 fusion.6
  74.5 0.4 fusion.25
  74.9 0.4 fusion.24
  75.3 0.4 fusion.5
  75.6 0.4 fusion.27
  76.0 0.4 fusion.26
  76.4 0.4 fusion.4
  76.8 0.4 fusion.29
  77.2 0.4 fusion.28
  77.6 0.4 fusion.3
  78.0 0.4 fusion.31
  78.4 0.4 fusion.30
  78.8 0.4 fusion.2
  79.1 0.4 fusion.33
  79.5 0.4 fusion.32
  79.9 0.4 fusion.1
  80.3 0.4 fusion.35
  80.7 0.4 fusion.34
  81.8 0.8 convolution_bitcast_fusion.1
  82.5 0.4 fusion
  82.9 0.4 convolution_divide_fusion
  83.3 0.3 convolution_bitcast_fusion.2
  83.6 0.3 fusion.36
  83.9 0.7 fusion.9
  84.6 7.0 %all_to_all.32 = f32[4,64,256]{2,1,0:T(8,128)S(1)} all-to-all(f32[4,64,256]{2,1,0:T(8,128)S(1)} %bitcast.106), channel_id=1, replica_groups=mesh['mem'=4,'reg'=8] {'mem'}, dimensions={0} | all-to-all | bytes 524288 | tf_op jit(solution)/shard_map/all_to_all | solution.py:79
  91.6 0.7 copy.23
  (6 shorter events, 0.1 us)
Async XLA Ops:
  6.5 40.5 %copy-start.3 = (f32[1024]{0:T(1024)S(1)}, f32[1024]{0:T(1024)}, u32[]{:S(2)}) copy-start(f32[1024]{0:T(1024)} %param.7) | copy-start | bytes 12292
  6.5 33.3 %all-gather.2.cloned.1.call-start = ((), (), s32[]{:S(2)}) async-start(), calls=%async_computation.2 | async-start | bytes 1310720 | tf_op jit(solution)/shard_map/all_gather | solution.py:64
  7.3 39.8 %collective-permute-start.2 = (f32[1,1024]{1,0:T(1,128)}, f32[1,1024]{1,0:T(1,128)S(1)}, u32[]{:S(2)}, u32[]{:S(2)}) collective-permute-start(f32[1,1024]{1,0:T(1,128)} %bitcast.114), channel_id=1, source_target_pairs={{0,1},{1,2},{2,3},{3,4},{4,5},{5,6},{6,7},{8,9},{9,10},{10,11},{11... | collective-permute-start | bytes 12296 | tf_op jit(solution)/shard_map/ppermute | solution.py:17
  11.9 35.2 %collective-permute-start.3 = (f32[1,1024]{1,0:T(1,128)}, f32[1,1024]{1,0:T(1,128)S(1)}, u32[]{:S(2)}, u32[]{:S(2)}) collective-permute-start(f32[1,1024]{1,0:T(1,128)} %bitcast.115), channel_id=1, source_target_pairs={{1,0},{2,1},{3,2},{4,3},{5,4},{6,5},{7,6},{9,8},{10,9},{11,10},{12... | collective-permute-start | bytes 12296 | tf_op jit(solution)/shard_map/ppermute | solution.py:19
  15.5 32.3 %all-to-all-start = ((f32[64,4,256]{2,0,1:T(8,128)}), f32[64,4,256]{2,0,1:T(8,128)S(1)}, u32[]{:S(2)}, u32[]{:S(2)}) async-start(f32[64,4,256]{2,0,1:T(8,128)} %bitcast.99), calls=%async_computation | async-start | bytes 524288 | tf_op jit(solution)/shard_map/all_to_all | solution.py:69
  41.4 15.4 %copy-start = (f32[256,1024]{0,1:T(8,128)}, f32[256,1024]{0,1:T(8,128)S(1)}, u32[]{:S(2)}) copy-start(f32[256,1024]{0,1:T(8,128)S(1)} %copy.15) | copy-start | bytes 3145732
  41.4 15.4 %collective-permute-start = (f32[256,1024]{0,1:T(8,128)S(1)}, f32[256,1024]{0,1:T(8,128)S(1)}, u32[]{:S(2)}, u32[]{:S(2)}) collective-permute-start(f32[256,1024]{0,1:T(8,128)S(1)} %copy.15), channel_id=1, source_target_pairs={{0,1},{1,2},{2,3},{3,4},{4,5},{5,6},{6,7},{8,9},{9,10},{10,11},{11... | collective-permute-start | bytes 3145736 | tf_op jit(solution)/shard_map/ppermute | solution.py:17
  45.1 16.2 %collective-permute-start.1 = (f32[256,1024]{0,1:T(8,128)S(1)}, f32[256,1024]{0,1:T(8,128)}, u32[]{:S(2)}, u32[]{:S(2)}) collective-permute-start(f32[256,1024]{0,1:T(8,128)S(1)} %copy.15), channel_id=1, source_target_pairs={{1,0},{2,1},{3,2},{4,3},{5,4},{6,5},{7,6},{9,8},{10,9},{11,10},{12... | collective-permute-start | bytes 3145736 | tf_op jit(solution)/shard_map/ppermute | solution.py:19
  56.8 1.0 copy-start.1
  68.2 0.8 copy-start.2
Sparse Core Ops, SparseCore 0:
  9.2 30.5 all-gather.1
where the time goes:
time: 99.6 us; the launch traced here: 99.2 us
  waiting for transfers between devices  33.4 us (34%)
  starting transfers between devices  15.5 us (16%)
  matrix products  14.7 us (15%)
  between operations  14.4 us (14%)
  local copies, waits for them, and re-layouts  11.1 us (11%)
  blocking collectives  6.96 us (7%)
  other arithmetic  3.04 us (3%)
    all_gather x1, waiting for transfers between devices, on_device(): whole = lax.all_gather(obs_pert, 'mem', axis=0, tiled=True)  20.2 us
    dot_general x28, matrix products, batched(): jnp.einsum(form, first, second, precision=lax.Precision.HIGHEST, preferre...  14.7 us
    ppermute x2, waiting for transfers between devices, extended(): lax.ppermute(tail, axis, [(i, (i + 1) % count) for i in range(ends)])  9.01 us
    ppermute x2, starting transfers between devices, extended(): lax.ppermute(tail, axis, [(i, (i + 1) % count) for i in range(ends)])  8.27 us
    all_to_all x1, blocking collectives, on_device(): lax.all_to_all(updated, 'mem', split_axis=0, concat_axis=1, tiled=True)  6.96 us
    ppermute x2, starting transfers between devices, extended(): lax.ppermute(head, axis, [((i + 1) % count, i) for i in range(ends)])  3.84 us
    ppermute x2, waiting for transfers between devices, extended(): lax.ppermute(head, axis, [((i + 1) % count, i) for i in range(ends)])  3.52 us
    all_to_all x1, starting transfers between devices, on_device(): lax.all_to_all(ensemble, 'mem', split_axis=1, concat_axis=0, tiled=True)  3.44 us
  transfers between devices with their start and end apart: 6, of which 3 were waited for; matrix products, arithmetic and copies ran while one was open for 5% of the time, Pallas kernels for 0%

commit v1 on v0

v1 whole, which is shorter than its diff:
```python
import functools

import jax
import jax.numpy as jnp
from jax import lax
from jax.experimental import pallas as pl
from jax.experimental.pallas import tpu as pltpu
from jax.sharding import PartitionSpec as P

NEWTON = 8
MESH = pl.DeviceIdType.MESH
NN = (((1,), (0,)), ((), ()))
NT = (((1,), (1,)), ((), ()))


def halves(value):
    high = value.astype(jnp.bfloat16)
    low = (value - high.astype(jnp.float32)).astype(jnp.bfloat16)
    return high, low


def product(first, second, dims=NN):
    dot = functools.partial(
        lax.dot_general, dimension_numbers=dims, preferred_element_type=jnp.float32
    )
    return dot(first[0], second[0]) + (dot(first[0], second[1]) + dot(first[1], second[0]))


def flipped(index, mask):
    bit = 1
    while bit <= mask:
        if mask & bit:
            index = index + bit * (1 - 2 * (lax.div(index, bit) % 2))
        bit *= 2
    return index


def kernel(
    n_mem, n_reg, block_ref, ens_ref, obs_ref, innov_ref, weight_ref, out_ref,
    obs_all, innov_all, columns, result, gram, drive_parts,
    local_sem, obs_send, obs_recv, halo_send, halo_recv, innov_send, innov_recv,
    ens_send, ens_recv, out_send, out_recv,
):
    me, region = lax.axis_index("mem"), lax.axis_index("reg")
    rows = obs_ref.shape[0]
    members = n_mem * rows
    own_obs = obs_ref.shape[1]
    points = columns.shape[1]
    listed, width = weight_ref.shape
    own_blocks = own_obs // width
    has_before, has_after = region > 0, region < n_reg - 1
    sides = ((has_before, region - 1, 0), (has_after, region + 1, 1))

    def rows_of(which):
        return pl.ds(pl.multiple_of(which * rows, rows), rows)

    def points_of(which):
        return pl.ds(pl.multiple_of(which * points, points), points)

    barrier = pltpu.get_barrier_semaphore()
    for step in range(1, n_mem):
        pl.semaphore_signal(
            barrier, inc=1, device_id=(flipped(me, step), region), device_id_type=MESH
        )
    for there, other, side in sides:
        @pl.when(there)
        def _():
            pl.semaphore_signal(barrier, inc=1, device_id=(me, other), device_id_type=MESH)

    own_obs_copy = pltpu.make_async_copy(obs_ref, obs_all.at[1, rows_of(me)], local_sem.at[0])
    own_obs_copy.start()
    own_innov_copy = pltpu.make_async_copy(innov_ref, innov_all.at[1], local_sem.at[1])
    own_innov_copy.start()
    own_ens_copy = pltpu.make_async_copy(
        ens_ref.at[:, points_of(me)], columns.at[rows_of(me)], local_sem.at[2]
    )
    own_ens_copy.start()

    near = has_before.astype(jnp.int32) + has_after.astype(jnp.int32)
    pl.semaphore_wait(barrier, n_mem - 1 + near)

    def gather(step):
        return pltpu.make_async_remote_copy(
            src_ref=obs_ref, dst_ref=obs_all.at[1, rows_of(me)],
            send_sem=obs_send.at[step], recv_sem=obs_recv.at[step],
            device_id=(flipped(me, step), region), device_id_type=MESH,
        )

    def halo(step, other, side):
        piece = rows_of(flipped(me, step))
        return pltpu.make_async_remote_copy(
            src_ref=obs_ref if step == 0 else obs_all.at[1, piece],
            dst_ref=obs_all.at[2 - 2 * side, piece],
            send_sem=halo_send.at[side, step], recv_sem=halo_recv.at[side, step],
            device_id=(me, other), device_id_type=MESH,
        )

    def innov(other, side):
        return pltpu.make_async_remote_copy(
            src_ref=innov_ref, dst_ref=innov_all.at[2 - 2 * side],
            send_sem=innov_send.at[side], recv_sem=innov_recv.at[side],
            device_id=(me, other), device_id_type=MESH,
        )

    def exchange(step):
        other = flipped(me, step)
        return pltpu.make_async_remote_copy(
            src_ref=ens_ref.at[:, points_of(other)], dst_ref=columns.at[rows_of(me)],
            send_sem=ens_send.at[step], recv_sem=ens_recv.at[step],
            device_id=(other, region), device_id_type=MESH,
        )

    def give_back(step):
        other = flipped(me, step)
        return pltpu.make_async_remote_copy(
            src_ref=result.at[rows_of(other)], dst_ref=out_ref.at[:, points_of(me)],
            send_sem=out_send.at[step], recv_sem=out_recv.at[step],
            device_id=(other, region), device_id_type=MESH,
        )

    for step in range(1, n_mem):
        gather(step).start()
    for there, other, side in sides:
        @pl.when(there)
        def _():
            halo(0, other, side).start()
            innov(other, side).start()
    for step in range(1, n_mem):
        exchange(step).start()
    for step in range(1, n_mem):
        gather(step).wait_recv()
        for there, other, side in sides:
            @pl.when(there)
            def _():
                halo(step, other, side).start()

    own_ens_copy.wait()
    for step in range(1, n_mem):
        exchange(step).wait_recv()
    ensemble = columns[...]
    mean = jnp.sum(ensemble, axis=0, keepdims=True) / members
    anomalies = ensemble - mean
    anomaly_halves = halves(anomalies)

    def add_region(slot):
        first = (region - 1 + slot) * own_blocks
        parts = []
        for at in range(own_blocks):
            chosen = jnp.where(block_ref[...] == first + at, weight_ref[...], 0.0)
            parts.append(jnp.sum(chosen, axis=0, keepdims=True))
        block = obs_all[slot]
        scaled = block * jnp.concatenate(parts, axis=1)
        gram[...] += product(halves(scaled), halves(block), NT)
        driven = scaled * innov_all[slot]
        total = driven[:, :width]
        for at in range(1, own_blocks):
            total = total + driven[:, at * width : (at + 1) * width]
        drive_parts[...] += total

    gram[...] = jnp.zeros_like(gram)
    drive_parts[...] = jnp.zeros_like(drive_parts)
    own_obs_copy.wait()
    own_innov_copy.wait()
    add_region(1)
    for there, other, side in sides:
        @pl.when(there)
        def _():
            for step in range(n_mem):
                halo(step, other, 1 - side).wait_recv()
            innov(other, 1 - side).wait_recv()
            add_region(2 * side)

    row_at = lax.broadcasted_iota(jnp.int32, (members, members), 0)
    column_at = lax.broadcasted_iota(jnp.int32, (members, members), 1)
    diagonal = row_at == column_at
    identity = jnp.where(diagonal, 1.0, 0.0)
    drive = jnp.sum(drive_parts[...], axis=1, keepdims=True)

    system = identity + gram[...] / (members - 1.0)
    trace = jnp.sum(jnp.where(diagonal, system, 0.0), axis=0, keepdims=True)
    trace = jnp.sum(trace, axis=1, keepdims=True)
    iterate_y = system / trace
    factor = 1.5 * identity - 0.5 * iterate_y
    factor_halves = halves(factor)
    iterate_y = product(halves(iterate_y), factor_halves)
    iterate_z = factor
    z_halves = factor_halves
    for repeat in range(1, NEWTON):
        y_halves = halves(iterate_y)
        factor_halves = halves(1.5 * identity - 0.5 * product(z_halves, y_halves))
        if repeat < NEWTON - 1:
            iterate_y = product(y_halves, factor_halves)
        iterate_z = product(factor_halves, z_halves)
        z_halves = halves(iterate_z)
    root = iterate_z * lax.rsqrt(trace)
    half_step = jnp.sum(root * drive, axis=0, keepdims=True)
    mean_weights = jnp.sum(root * half_step, axis=1, keepdims=True) / (members - 1.0)
    shift = mean + jnp.sum(anomalies * mean_weights, axis=0, keepdims=True)
    result[...] = shift + product(halves(root), anomaly_halves)

    for step in range(1, n_mem):
        give_back(step).start()
    own_out = pltpu.make_async_copy(
        result.at[rows_of(me)], out_ref.at[:, points_of(me)], local_sem.at[3]
    )
    own_out.start()
    for step in range(1, n_mem):
        gather(step).wait_send()
        exchange(step).wait_send()
    for there, other, side in sides:
        @pl.when(there)
        def _():
            for step in range(n_mem):
                halo(step, other, side).wait_send()
            innov(other, side).wait_send()
    own_out.wait()
    for step in range(1, n_mem):
        give_back(step).wait()


def on_device(ensemble, obs_pert, innovation, block_list, loc_weights):
    n_mem, n_reg = lax.axis_size("mem"), lax.axis_size("reg")
    rows, own_points = ensemble.shape
    own_obs = obs_pert.shape[1]
    listed, width = loc_weights.shape[1:]
    members, points = rows * n_mem, own_points // n_mem
    return pl.pallas_call(
        functools.partial(kernel, n_mem, n_reg),
        out_shape=jax.ShapeDtypeStruct((rows, own_points), jnp.float32),
        in_specs=[
            pl.BlockSpec(memory_space=pltpu.VMEM),
            pl.BlockSpec(memory_space=pl.ANY),
            pl.BlockSpec(memory_space=pl.ANY),
            pl.BlockSpec(memory_space=pltpu.VMEM),
            pl.BlockSpec(memory_space=pltpu.VMEM),
        ],
        out_specs=pl.BlockSpec(memory_space=pl.ANY),
        scratch_shapes=[
            pltpu.VMEM((3, members, own_obs), jnp.float32),
            pltpu.VMEM((3, 1, own_obs), jnp.float32),
            pltpu.VMEM((members, points), jnp.float32),
            pltpu.VMEM((members, points), jnp.float32),
            pltpu.VMEM((members, members), jnp.float32),
            pltpu.VMEM((members, width), jnp.float32),
            pltpu.SemaphoreType.DMA((4,)),
            pltpu.SemaphoreType.DMA((n_mem,)),
            pltpu.SemaphoreType.DMA((n_mem,)),
            pltpu.SemaphoreType.DMA((2, n_mem)),
            pltpu.SemaphoreType.DMA((2, n_mem)),
            pltpu.SemaphoreType.DMA((2,)),
            pltpu.SemaphoreType.DMA((2,)),
            pltpu.SemaphoreType.DMA((n_mem,)),
            pltpu.SemaphoreType.DMA((n_mem,)),
            pltpu.SemaphoreType.DMA((n_mem,)),
            pltpu.SemaphoreType.DMA((n_mem,)),
        ],
        compiler_params=pltpu.CompilerParams(
            collective_id=0, has_side_effects=True, vmem_limit_bytes=32 * 2**20
        ),
    )(
        block_list.reshape(listed, 1), ensemble, obs_pert,
        innovation.reshape(1, own_obs), loc_weights.reshape(listed, width),
    )


def solution(mesh):
    return jax.shard_map(
        on_device,
        mesh=mesh,
        in_specs=(
            P("mem", "reg"),
            P("mem", "reg"),
            P("reg"),
            P(("reg", "mem"), None),
            P(("reg", "mem"), None, None),
        ),
        out_specs=P("mem", "reg"),
        check_vma=False,
    )
```

time: 99.6 us -> 37.7 us (0.38)
  Pallas kernels: 0 us -> 34.1 us
  waiting for transfers between devices: 33.4 us -> 0 us
  starting transfers between devices: 15.5 us -> 0 us
  matrix products: 14.7 us -> 0 us
  between operations: 14.4 us -> 0.02 us
  local copies, waits for them, and re-layouts: 11.1 us -> 3.34 us
  blocking collectives: 6.96 us -> 0 us
  other arithmetic: 3.04 us -> 0 us
    pallas_call x0 -> x1, Pallas kernels: none -> 34.1 us  [on_device(): pl.pallas_call(functools.partial(kernel, n_mem, n_reg), out_shape=jax.Sha...]
    all_gather x1 -> x0, waiting for transfers between devices: 20.2 us -> none  [on_device(): whole = lax.all_gather(obs_pert, 'mem', axis=0, tiled=True)]
    dot_general x28 -> x0, matrix products: 14.7 us -> none  [batched(): jnp.einsum(form, first, second, precision=lax.Precision.HIGHEST, preferre...]
    ppermute x4 -> x0, waiting for transfers between devices: 12.5 us -> none  [the longest x2 9.01 us: extended(): lax.ppermute(tail, axis, [(i, (i + 1) % count) for i in range(ends)])]
    ppermute x4 -> x0, starting transfers between devices: 12.1 us -> none  [the longest x2 8.27 us: extended(): lax.ppermute(tail, axis, [(i, (i + 1) % count) for i in range(ends)])]
    all_to_all x1 -> x0, blocking collectives: 6.96 us -> none  [on_device(): lax.all_to_all(updated, 'mem', split_axis=0, concat_axis=1, tiled=True)]
    all_to_all x1 -> x0, starting transfers between devices: 3.44 us -> none  [on_device(): lax.all_to_all(ensemble, 'mem', split_axis=1, concat_axis=0, tiled=True)]
    gather x3 -> x0, local copies, waits for them, and re-layouts: 3.39 us -> none  [the longest x2 2.83 us: on_device(): jnp.take(edged_blocks, local_blocks, axis=1)]
  transfers between devices with their start and end apart: 6 -> 0, of which waited for: 3 -> 0; matrix products, arithmetic and copies ran while one was open for 5% -> 0% of each run, Pallas kernels for 0% -> 0%
where the time goes in v1:
time: 37.7 us; the launch traced here: 37.5 us
  Pallas kernels  34.1 us (90%)
  local copies, waits for them, and re-layouts  3.34 us (9%)
    pallas_call x1, Pallas kernels, on_device(): pl.pallas_call(functools.partial(kernel, n_mem, n_reg), out_shape=jax.Sha...  34.1 us
    unnamed x11, local copies, waits for them, and re-layouts  3.26 us

profile of v1, /device:TPU:1, one launch (start us, length us, event | category | flops | bytes accessed | tf_op | source)
XLA Modules:
  0.0 37.5 jit_solution(2762996534156335594)
XLA Ops:
  0.0 0.0 copy-start.4
  0.0 0.0 copy-start.2
  0.0 0.0 copy-start.3
  0.0 0.6 %copy-done.4 = s32[1,8]{1,0:T(1,128)S(1)} copy-done((s32[1,8]{1,0:T(1,128)S(1)}, s32[1,8]{1,0:T(1,128)}, u32[]{:S(2)}) %copy-start.4) | copy-done | bytes 56
  0.7 0.1 copy.6.block_ref
  0.7 0.0 copy-done.2
  0.7 0.0 copy-done.3
  0.7 0.0 copy-start
  0.7 0.9 %copy-done = f32[64,1024]{1,0:T(8,128)S(1)} copy-done((f32[64,1024]{1,0:T(8,128)S(1)}, f32[64,1024]{1,0:T(8,128)}, u32[]{:S(2)}) %copy-start) | copy-done | bytes 262168
  1.7 0.0 copy-start.1
  1.7 0.9 %copy-done.1 = f32[64,1024]{1,0:T(8,128)S(1)} copy-done((f32[64,1024]{1,0:T(8,128)S(1)}, f32[64,1024]{1,0:T(8,128)}, u32[]{:S(2)}) %copy-start.1) | copy-done | bytes 262168
  2.6 34.1 %shard_map.55 = f32[64,1024]{1,0:T(8,128)S(1)} custom-call(s32[8,1]{1,0:T(8,128)S(1)} %copy.6.block_ref, f32[64,1024]{1,0:T(8,128)S(1)} %copy-done, f32[64,1024]{1,0:T(8,128)S(1)} %copy-done.1, f32[1,1024]{1,0:T(1,128)S(1)} %bitcast.3, f32[8,128]{1,0:T(8,128)S(1)} %bitcast.4), custom_call_target="tpu_custom_call" | custom-call | tf_op jit(solution)/shard_map/pallas_call | solution.py:227
  36.7 0.7 %copy.8 = f32[64,1024]{1,0:T(8,128)} copy(f32[64,1024]{1,0:T(8,128)S(1)} %shard_map.55) | data formatting | bytes 524288
Async XLA Ops:
  0.0 0.7 %copy-start.4 = (s32[1,8]{1,0:T(1,128)S(1)}, s32[1,8]{1,0:T(1,128)}, u32[]{:S(2)}) copy-start(s32[1,8]{1,0:T(1,128)} %param.8) | copy-start | bytes 100
  0.0 0.7 %copy-start.2 = (f32[1024]{0:T(1024)S(1)}, f32[1024]{0:T(1024)}, u32[]{:S(2)}) copy-start(f32[1024]{0:T(1024)} %param.7) | copy-start | bytes 12292
  0.0 0.7 %copy-start.3 = (f32[1,8,128]{2,1,0:T(8,128)S(1)}, f32[1,8,128]{2,1,0:T(8,128)}, u32[]{:S(2)}) copy-start(f32[1,8,128]{2,1,0:T(8,128)} %param.9) | copy-start | bytes 12292
  0.7 1.0 %copy-start = (f32[64,1024]{1,0:T(8,128)S(1)}, f32[64,1024]{1,0:T(8,128)}, u32[]{:S(2)}) copy-start(f32[64,1024]{1,0:T(8,128)} %ens_ref.1) | copy-start | bytes 786436
  1.7 0.9 %copy-start.1 = (f32[64,1024]{1,0:T(8,128)S(1)}, f32[64,1024]{1,0:T(8,128)}, u32[]{:S(2)}) copy-start(f32[64,1024]{1,0:T(8,128)} %obs_ref.1) | copy-start | bytes 786436

commit v2 on v1

--- a/solution.py
+++ b/solution.py
@@ -255,7 +255,7 @@
             pltpu.SemaphoreType.DMA((n_mem,)),
         ],
         compiler_params=pltpu.CompilerParams(
-            collective_id=0, has_side_effects=True, vmem_limit_bytes=32 * 2**20
+            collective_id=0, has_side_effects=True, vmem_limit_bytes=60 * 2**20
         ),
     )(
         block_list.reshape(listed, 1), ensemble, obs_pert,

time: 37.7 us -> 38.7 us (1.027)
  Pallas kernels: 34.1 us -> 35.5 us
    pallas_call x1, Pallas kernels: 34.1 us -> 35.5 us  [on_device(): pl.pallas_call(functools.partial(kernel, n_mem, n_reg), out_shape=jax.Sha...]
    unnamed x11 -> x3, local copies, waits for them, and re-layouts: 3.26 us -> 2.33 us
    reshape x1, local copies, waits for them, and re-layouts: 0.08 us -> 0.67 us  [on_device(): block_list.reshape(listed, 1)]
where the time goes in v2:
time: 38.7 us; the launch traced here: 38.5 us
  Pallas kernels  35.5 us (92%)
  local copies, waits for them, and re-layouts  3 us (8%)
    pallas_call x1, Pallas kernels, on_device(): pl.pallas_call(functools.partial(kernel, n_mem, n_reg), out_shape=jax.Sha...  35.5 us
    unnamed x3, local copies, waits for them, and re-layouts  2.33 us

profile of v2, /device:TPU:1, one launch (start us, length us, event | category | flops | bytes accessed | tf_op | source)
XLA Modules:
  0.0 38.5 jit_solution(2938159213870170280)
XLA Ops:
  0.0 0.0 copy-start
  0.0 0.7 %copy-done = s32[1,8]{1,0:T(1,128)S(1)} copy-done((s32[1,8]{1,0:T(1,128)S(1)}, s32[1,8]{1,0:T(1,128)}, u32[]{:S(2)}) %copy-start) | copy-done | bytes 56
  0.7 0.7 %copy.6.block_ref = s32[8,1]{1,0:T(8,128)} copy(s32[8,1]{0,1:T(1,128)S(1)} %bitcast.5) | data formatting | bytes 64 | tf_op jit(solution)/shard_map/reshape | solution.py:261
  1.3 35.5 %shard_map.55 = f32[64,1024]{1,0:T(8,128)} custom-call(s32[8,1]{1,0:T(8,128)} %copy.6.block_ref, f32[64,1024]{1,0:T(8,128)} %ens_ref.1, f32[64,1024]{1,0:T(8,128)} %obs_ref.1, f32[1,1024]{1,0:T(1,128)} %bitcast.3, f32[8,128]{1,0:T(8,128)} %bitcast.4), custom_call_target="tpu_custom_call" | custom-call | tf_op jit(solution)/shard_map/pallas_call | solution.py:227
  36.8 1.7 %copy.8 = f32[64,1024]{1,0:T(8,128)} copy(f32[64,1024]{1,0:T(8,128)} %shard_map.55) | data formatting | bytes 524288
Async XLA Ops:
  0.0 0.7 %copy-start = (s32[1,8]{1,0:T(1,128)S(1)}, s32[1,8]{1,0:T(1,128)}, u32[]{:S(2)}) copy-start(s32[1,8]{1,0:T(1,128)} %param.8) | copy-start | bytes 100

commit v3 on v1

--- a/solution.py
+++ b/solution.py
@@ -54,6 +54,12 @@
     def rows_of(which):
         return pl.ds(pl.multiple_of(which * rows, rows), rows)
 
+    parts_in = obs_send.shape[1]
+    part = rows // parts_in
+
+    def part_of(which, at):
+        return pl.ds(pl.multiple_of(which * rows + at * part, part), part)
+
     def points_of(which):
         return pl.ds(pl.multiple_of(which * points, points), points)
 
@@ -79,19 +85,19 @@
     near = has_before.astype(jnp.int32) + has_after.astype(jnp.int32)
     pl.semaphore_wait(barrier, n_mem - 1 + near)
 
-    def gather(step):
-        return pltpu.make_async_remote_copy(
-            src_ref=obs_ref, dst_ref=obs_all.at[1, rows_of(me)],
-            send_sem=obs_send.at[step], recv_sem=obs_recv.at[step],
+    def gather(step, at):
+        return pltpu.make_async_remote_copy(
+            src_ref=obs_ref.at[pl.ds(at * part, part)], dst_ref=obs_all.at[1, part_of(me, at)],
+            send_sem=obs_send.at[step, at], recv_sem=obs_recv.at[step, at],
             device_id=(flipped(me, step), region), device_id_type=MESH,
         )
 
-    def halo(step, other, side):
-        piece = rows_of(flipped(me, step))
-        return pltpu.make_async_remote_copy(
-            src_ref=obs_ref if step == 0 else obs_all.at[1, piece],
+    def halo(step, at, other, side):
+        piece = part_of(flipped(me, step), at)
+        return pltpu.make_async_remote_copy(
+            src_ref=obs_ref.at[pl.ds(at * part, part)] if step == 0 else obs_all.at[1, piece],
             dst_ref=obs_all.at[2 - 2 * side, piece],
-            send_sem=halo_send.at[side, step], recv_sem=halo_recv.at[side, step],
+            send_sem=halo_send.at[side, step, at], recv_sem=halo_recv.at[side, step, at],
             device_id=(me, other), device_id_type=MESH,
         )
 
@@ -118,21 +124,24 @@
             device_id=(other, region), device_id_type=MESH,
         )
 
-    for step in range(1, n_mem):
-        gather(step).start()
-    for there, other, side in sides:
-        @pl.when(there)
-        def _():
-            halo(0, other, side).start()
+    for at in range(parts_in):
+        for step in range(1, n_mem):
+            gather(step, at).start()
+    for there, other, side in sides:
+        @pl.when(there)
+        def _():
+            for at in range(parts_in):
+                halo(0, at, other, side).start()
             innov(other, side).start()
     for step in range(1, n_mem):
         exchange(step).start()
-    for step in range(1, n_mem):
-        gather(step).wait_recv()
-        for there, other, side in sides:
-            @pl.when(there)
-            def _():
-                halo(step, other, side).start()
+    for at in range(parts_in):
+        for step in range(1, n_mem):
+            gather(step, at).wait_recv()
+            for there, other, side in sides:
+                @pl.when(there)
+                def _():
+                    halo(step, at, other, side).start()
 
     own_ens_copy.wait()
     for step in range(1, n_mem):
@@ -166,7 +175,8 @@
         @pl.when(there)
         def _():
             for step in range(n_mem):
-                halo(step, other, 1 - side).wait_recv()
+                for at in range(parts_in):
+                    halo(step, at, other, 1 - side).wait_recv()
             innov(other, 1 - side).wait_recv()
             add_region(2 * side)
 
@@ -205,13 +215,15 @@
     )
     own_out.start()
     for step in range(1, n_mem):
-        gather(step).wait_send()
+        for at in range(parts_in):
+            gather(step, at).wait_send()
         exchange(step).wait_send()
     for there, other, side in sides:
         @pl.when(there)
         def _():
             for step in range(n_mem):
-                halo(step, other, side).wait_send()
+                for at in range(parts_in):
+                    halo(step, at, other, side).wait_send()
             innov(other, side).wait_send()
     own_out.wait()
     for step in range(1, n_mem):
@@ -224,6 +236,7 @@
     own_obs = obs_pert.shape[1]
     listed, width = loc_weights.shape[1:]
     members, points = rows * n_mem, own_points // n_mem
+    parts_in = 2 if rows % 16 == 0 else 1
     return pl.pallas_call(
         functools.partial(kernel, n_mem, n_reg),
         out_shape=jax.ShapeDtypeStruct((rows, own_points), jnp.float32),
@@ -243,10 +256,10 @@
             pltpu.VMEM((members, members), jnp.float32),
             pltpu.VMEM((members, width), jnp.float32),
             pltpu.SemaphoreType.DMA((4,)),
-            pltpu.SemaphoreType.DMA((n_mem,)),
-            pltpu.SemaphoreType.DMA((n_mem,)),
-            pltpu.SemaphoreType.DMA((2, n_mem)),
-            pltpu.SemaphoreType.DMA((2, n_mem)),
+            pltpu.SemaphoreType.DMA((n_mem, parts_in)),
+            pltpu.SemaphoreType.DMA((n_mem, parts_in)),
+            pltpu.SemaphoreType.DMA((2, n_mem, parts_in)),
+            pltpu.SemaphoreType.DMA((2, n_mem, parts_in)),
             pltpu.SemaphoreType.DMA((2,)),
             pltpu.SemaphoreType.DMA((2,)),
             pltpu.SemaphoreType.DMA((n_mem,)),

time: 37.7 us -> 35.9 us (0.952)
  Pallas kernels: 34.1 us -> 32.3 us
    pallas_call x1, Pallas kernels: 34.1 us -> 32.3 us  [on_device(): pl.pallas_call(functools.partial(kernel, n_mem, n_reg), out_shape=jax.Sha...]
where the time goes in v3:
time: 35.9 us; the launch traced here: 35.7 us
  Pallas kernels  32.3 us (90%)
  local copies, waits for them, and re-layouts  3.34 us (9%)
    pallas_call x1, Pallas kernels, on_device(): pl.pallas_call(functools.partial(kernel, n_mem, n_reg), out_shape=jax.Sha...  32.3 us
    unnamed x11, local copies, waits for them, and re-layouts  3.26 us

profile of v3, /device:TPU:1, one launch (start us, length us, event | category | flops | bytes accessed | tf_op | source)
XLA Modules:
  0.0 35.7 jit_solution(10030351514864133000)
XLA Ops:
  0.0 0.0 copy-start.4
  0.0 0.0 copy-start.2
  0.0 0.0 copy-start.3
  0.0 0.6 %copy-done.4 = s32[1,8]{1,0:T(1,128)S(1)} copy-done((s32[1,8]{1,0:T(1,128)S(1)}, s32[1,8]{1,0:T(1,128)}, u32[]{:S(2)}) %copy-start.4) | copy-done | bytes 56
  0.7 0.1 copy.6.block_ref
  0.7 0.0 copy-done.2
  0.7 0.0 copy-done.3
  0.7 0.0 copy-start
  0.7 0.9 %copy-done = f32[64,1024]{1,0:T(8,128)S(1)} copy-done((f32[64,1024]{1,0:T(8,128)S(1)}, f32[64,1024]{1,0:T(8,128)}, u32[]{:S(2)}) %copy-start) | copy-done | bytes 262168
  1.7 0.0 copy-start.1
  1.7 0.9 %copy-done.1 = f32[64,1024]{1,0:T(8,128)S(1)} copy-done((f32[64,1024]{1,0:T(8,128)S(1)}, f32[64,1024]{1,0:T(8,128)}, u32[]{:S(2)}) %copy-start.1) | copy-done | bytes 262168
  2.6 32.3 %shard_map.55 = f32[64,1024]{1,0:T(8,128)S(1)} custom-call(s32[8,1]{1,0:T(8,128)S(1)} %copy.6.block_ref, f32[64,1024]{1,0:T(8,128)S(1)} %copy-done, f32[64,1024]{1,0:T(8,128)S(1)} %copy-done.1, f32[1,1024]{1,0:T(1,128)S(1)} %bitcast.3, f32[8,128]{1,0:T(8,128)S(1)} %bitcast.4), custom_call_target="tpu_custom_call" | custom-call | tf_op jit(solution)/shard_map/pallas_call | solution.py:240
  35.0 0.7 %copy.8 = f32[64,1024]{1,0:T(8,128)} copy(f32[64,1024]{1,0:T(8,128)S(1)} %shard_map.55) | data formatting | bytes 524288
Async XLA Ops:
  0.0 0.7 %copy-start.4 = (s32[1,8]{1,0:T(1,128)S(1)}, s32[1,8]{1,0:T(1,128)}, u32[]{:S(2)}) copy-start(s32[1,8]{1,0:T(1,128)} %param.8) | copy-start | bytes 100
  0.0 0.7 %copy-start.2 = (f32[1024]{0:T(1024)S(1)}, f32[1024]{0:T(1024)}, u32[]{:S(2)}) copy-start(f32[1024]{0:T(1024)} %param.7) | copy-start | bytes 12292
  0.0 0.7 %copy-start.3 = (f32[1,8,128]{2,1,0:T(8,128)S(1)}, f32[1,8,128]{2,1,0:T(8,128)}, u32[]{:S(2)}) copy-start(f32[1,8,128]{2,1,0:T(8,128)} %param.9) | copy-start | bytes 12292
  0.7 1.0 %copy-start = (f32[64,1024]{1,0:T(8,128)S(1)}, f32[64,1024]{1,0:T(8,128)}, u32[]{:S(2)}) copy-start(f32[64,1024]{1,0:T(8,128)} %ens_ref.1) | copy-start | bytes 786436
  1.7 0.9 %copy-start.1 = (f32[64,1024]{1,0:T(8,128)S(1)}, f32[64,1024]{1,0:T(8,128)}, u32[]{:S(2)}) copy-start(f32[64,1024]{1,0:T(8,128)} %obs_ref.1) | copy-start | bytes 786436

commit v4 on v3

--- a/solution.py
+++ b/solution.py
@@ -24,6 +24,19 @@
         lax.dot_general, dimension_numbers=dims, preferred_element_type=jnp.float32
     )
     return dot(first[0], second[0]) + (dot(first[0], second[1]) + dot(first[1], second[0]))
+
+
+def stacked(firsts, second):
+    dot = functools.partial(jnp.dot, preferred_element_type=jnp.float32)
+    size, count = second[0].shape[0], len(firsts)
+    highs = [first[0] for first in firsts]
+    wide = dot(jnp.concatenate(highs + [first[1] for first in firsts], axis=0), second[0])
+    thin = dot(jnp.concatenate(highs, axis=0) if count > 1 else highs[0], second[1])
+    return [
+        wide[at * size : (at + 1) * size]
+        + (thin[at * size : (at + 1) * size] + wide[(count + at) * size : (count + at + 1) * size])
+        for at in range(count)
+    ]
 
 
 def flipped(index, mask):
@@ -192,16 +205,18 @@
     iterate_y = system / trace
     factor = 1.5 * identity - 0.5 * iterate_y
     factor_halves = halves(factor)
-    iterate_y = product(halves(iterate_y), factor_halves)
+    [iterate_y] = stacked([halves(iterate_y)], factor_halves)
     iterate_z = factor
     z_halves = factor_halves
     for repeat in range(1, NEWTON):
         y_halves = halves(iterate_y)
-        factor_halves = halves(1.5 * identity - 0.5 * product(z_halves, y_halves))
+        [both] = stacked([z_halves], y_halves)
+        factor_halves = halves(1.5 * identity - 0.5 * both)
         if repeat < NEWTON - 1:
-            iterate_y = product(y_halves, factor_halves)
-        iterate_z = product(factor_halves, z_halves)
-        z_halves = halves(iterate_z)
+            iterate_y, iterate_z = stacked([y_halves, z_halves], factor_halves)
+            z_halves = halves(iterate_z)
+        else:
+            [iterate_z] = stacked([z_halves], factor_halves)
     root = iterate_z * lax.rsqrt(trace)
     half_step = jnp.sum(root * drive, axis=0, keepdims=True)
     mean_weights = jnp.sum(root * half_step, axis=1, keepdims=True) / (members - 1.0)

time: 35.9 us -> 36.7 us (1.022)
  Pallas kernels: 32.3 us -> 33.2 us
    pallas_call x1, Pallas kernels: 32.3 us -> 33.2 us  [on_device(): pl.pallas_call(functools.partial(kernel, n_mem, n_reg), out_shape=jax.Sha...]
where the time goes in v4:
time: 36.7 us; the launch traced here: 36.5 us
  Pallas kernels  33.2 us (90%)
  local copies, waits for them, and re-layouts  3.34 us (9%)
    pallas_call x1, Pallas kernels, on_device(): pl.pallas_call(functools.partial(kernel, n_mem, n_reg), out_shape=jax.Sha...  33.2 us
    unnamed x11, local copies, waits for them, and re-layouts  3.26 us

profile of v4, /device:TPU:1, one launch (start us, length us, event | category | flops | bytes accessed | tf_op | source)
XLA Modules:
  0.0 36.5 jit_solution(5447979163569763552)
XLA Ops:
  0.0 0.0 copy-start.4
  0.0 0.0 copy-start.2
  0.0 0.0 copy-start.3
  0.0 0.6 %copy-done.4 = s32[1,8]{1,0:T(1,128)S(1)} copy-done((s32[1,8]{1,0:T(1,128)S(1)}, s32[1,8]{1,0:T(1,128)}, u32[]{:S(2)}) %copy-start.4) | copy-done | bytes 56
  0.7 0.1 copy.6.block_ref
  0.7 0.0 copy-done.2
  0.7 0.0 copy-done.3
  0.7 0.0 copy-start
  0.7 0.9 %copy-done = f32[64,1024]{1,0:T(8,128)S(1)} copy-done((f32[64,1024]{1,0:T(8,128)S(1)}, f32[64,1024]{1,0:T(8,128)}, u32[]{:S(2)}) %copy-start) | copy-done | bytes 262168
  1.7 0.0 copy-start.1
  1.7 0.9 %copy-done.1 = f32[64,1024]{1,0:T(8,128)S(1)} copy-done((f32[64,1024]{1,0:T(8,128)S(1)}, f32[64,1024]{1,0:T(8,128)}, u32[]{:S(2)}) %copy-start.1) | copy-done | bytes 262168
  2.6 33.2 %shard_map.55 = f32[64,1024]{1,0:T(8,128)S(1)} custom-call(s32[8,1]{1,0:T(8,128)S(1)} %copy.6.block_ref, f32[64,1024]{1,0:T(8,128)S(1)} %copy-done, f32[64,1024]{1,0:T(8,128)S(1)} %copy-done.1, f32[1,1024]{1,0:T(1,128)S(1)} %bitcast.3, f32[8,128]{1,0:T(8,128)S(1)} %bitcast.4), custom_call_target="tpu_custom_call" | custom-call | tf_op jit(solution)/shard_map/pallas_call | solution.py:255
  35.8 0.7 %copy.8 = f32[64,1024]{1,0:T(8,128)} copy(f32[64,1024]{1,0:T(8,128)S(1)} %shard_map.55) | data formatting | bytes 524288
Async XLA Ops:
  0.0 0.7 %copy-start.4 = (s32[1,8]{1,0:T(1,128)S(1)}, s32[1,8]{1,0:T(1,128)}, u32[]{:S(2)}) copy-start(s32[1,8]{1,0:T(1,128)} %param.8) | copy-start | bytes 100
  0.0 0.7 %copy-start.2 = (f32[1024]{0:T(1024)S(1)}, f32[1024]{0:T(1024)}, u32[]{:S(2)}) copy-start(f32[1024]{0:T(1024)} %param.7) | copy-start | bytes 12292
  0.0 0.7 %copy-start.3 = (f32[1,8,128]{2,1,0:T(8,128)S(1)}, f32[1,8,128]{2,1,0:T(8,128)}, u32[]{:S(2)}) copy-start(f32[1,8,128]{2,1,0:T(8,128)} %param.9) | copy-start | bytes 12292
  0.7 1.0 %copy-start = (f32[64,1024]{1,0:T(8,128)S(1)}, f32[64,1024]{1,0:T(8,128)}, u32[]{:S(2)}) copy-start(f32[64,1024]{1,0:T(8,128)} %ens_ref.1) | copy-start | bytes 786436
  1.7 0.9 %copy-start.1 = (f32[64,1024]{1,0:T(8,128)S(1)}, f32[64,1024]{1,0:T(8,128)}, u32[]{:S(2)}) copy-start(f32[64,1024]{1,0:T(8,128)} %obs_ref.1) | copy-start | bytes 786436

commit v5 on v3

--- a/solution.py
+++ b/solution.py
@@ -85,7 +85,18 @@
     near = has_before.astype(jnp.int32) + has_after.astype(jnp.int32)
     pl.semaphore_wait(barrier, n_mem - 1 + near)
 
+    relay = n_mem == 4 and parts_in > 1
+    direct = n_mem - 1 if relay else n_mem
+
     def gather(step, at):
+        if relay and step == 3:
+            source, target = (2, 1) if at % 2 == 0 else (1, 2)
+            piece = part_of(flipped(me, source), at)
+            return pltpu.make_async_remote_copy(
+                src_ref=obs_all.at[1, piece], dst_ref=obs_all.at[1, piece],
+                send_sem=obs_send.at[step, at], recv_sem=obs_recv.at[step, at],
+                device_id=(flipped(me, target), region), device_id_type=MESH,
+            )
         return pltpu.make_async_remote_copy(
             src_ref=obs_ref.at[pl.ds(at * part, part)], dst_ref=obs_all.at[1, part_of(me, at)],
             send_sem=obs_send.at[step, at], recv_sem=obs_recv.at[step, at],
@@ -125,7 +136,7 @@
         )
 
     for at in range(parts_in):
-        for step in range(1, n_mem):
+        for step in range(1, direct):
             gather(step, at).start()
     for there, other, side in sides:
         @pl.when(there)
@@ -135,13 +146,21 @@
             innov(other, side).start()
     for step in range(1, n_mem):
         exchange(step).start()
+    def pass_on(step, at):
+        gather(step, at).wait_recv()
+        if relay and (step == 1 and at % 2 == 1 or step == 2 and at % 2 == 0):
+            gather(3, at).start()
+        for there, other, side in sides:
+            @pl.when(there)
+            def _():
+                halo(step, at, other, side).start()
+
     for at in range(parts_in):
-        for step in range(1, n_mem):
-            gather(step, at).wait_recv()
-            for there, other, side in sides:
-                @pl.when(there)
-                def _():
-                    halo(step, at, other, side).start()
+        for step in range(1, direct):
+            pass_on(step, at)
+    for at in range(parts_in):
+        for step in range(direct, n_mem):
+            pass_on(step, at)
 
     own_ens_copy.wait()
     for step in range(1, n_mem):
@@ -236,7 +255,7 @@
     own_obs = obs_pert.shape[1]
     listed, width = loc_weights.shape[1:]
     members, points = rows * n_mem, own_points // n_mem
-    parts_in = 2 if rows % 16 == 0 else 1
+    parts_in = 4 if rows % 32 == 0 else 2 if rows % 16 == 0 else 1
     return pl.pallas_call(
         functools.partial(kernel, n_mem, n_reg),
         out_shape=jax.ShapeDtypeStruct((rows, own_points), jnp.float32),

time: 35.9 us -> 35.1 us (0.978)
  Pallas kernels: 32.3 us -> 31.6 us
    pallas_call x1, Pallas kernels: 32.3 us -> 31.6 us  [on_device(): pl.pallas_call(functools.partial(kernel, n_mem, n_reg), out_shape=jax.Sha...]
where the time goes in v5:
time: 35.1 us; the launch traced here: 34.9 us
  Pallas kernels  31.6 us (90%)
  local copies, waits for them, and re-layouts  3.34 us (10%)
    pallas_call x1, Pallas kernels, on_device(): pl.pallas_call(functools.partial(kernel, n_mem, n_reg), out_shape=jax.Sha...  31.6 us
    unnamed x11, local copies, waits for them, and re-layouts  3.26 us

profile of v5, /device:TPU:1, one launch (start us, length us, event | category | flops | bytes accessed | tf_op | source)
XLA Modules:
  0.0 34.9 jit_solution(7209008655813219706)
XLA Ops:
  0.0 0.0 copy-start.4
  0.0 0.0 copy-start.2
  0.0 0.0 copy-start.3
  0.0 0.6 %copy-done.4 = s32[1,8]{1,0:T(1,128)S(1)} copy-done((s32[1,8]{1,0:T(1,128)S(1)}, s32[1,8]{1,0:T(1,128)}, u32[]{:S(2)}) %copy-start.4) | copy-done | bytes 56
  0.7 0.1 copy.6.block_ref
  0.7 0.0 copy-done.2
  0.7 0.0 copy-done.3
  0.7 0.0 copy-start
  0.7 0.9 %copy-done = f32[64,1024]{1,0:T(8,128)S(1)} copy-done((f32[64,1024]{1,0:T(8,128)S(1)}, f32[64,1024]{1,0:T(8,128)}, u32[]{:S(2)}) %copy-start) | copy-done | bytes 262168
  1.7 0.0 copy-start.1
  1.7 0.9 %copy-done.1 = f32[64,1024]{1,0:T(8,128)S(1)} copy-done((f32[64,1024]{1,0:T(8,128)S(1)}, f32[64,1024]{1,0:T(8,128)}, u32[]{:S(2)}) %copy-start.1) | copy-done | bytes 262168
  2.6 31.6 %shard_map.55 = f32[64,1024]{1,0:T(8,128)S(1)} custom-call(s32[8,1]{1,0:T(8,128)S(1)} %copy.6.block_ref, f32[64,1024]{1,0:T(8,128)S(1)} %copy-done, f32[64,1024]{1,0:T(8,128)S(1)} %copy-done.1, f32[1,1024]{1,0:T(1,128)S(1)} %bitcast.3, f32[8,128]{1,0:T(8,128)S(1)} %bitcast.4), custom_call_target="tpu_custom_call" | custom-call | tf_op jit(solution)/shard_map/pallas_call | solution.py:259
  34.2 0.7 %copy.8 = f32[64,1024]{1,0:T(8,128)} copy(f32[64,1024]{1,0:T(8,128)S(1)} %shard_map.55) | data formatting | bytes 524288
Async XLA Ops:
  0.0 0.7 %copy-start.4 = (s32[1,8]{1,0:T(1,128)S(1)}, s32[1,8]{1,0:T(1,128)}, u32[]{:S(2)}) copy-start(s32[1,8]{1,0:T(1,128)} %param.8) | copy-start | bytes 100
  0.0 0.7 %copy-start.2 = (f32[1024]{0:T(1024)S(1)}, f32[1024]{0:T(1024)}, u32[]{:S(2)}) copy-start(f32[1024]{0:T(1024)} %param.7) | copy-start | bytes 12292
  0.0 0.7 %copy-start.3 = (f32[1,8,128]{2,1,0:T(8,128)S(1)}, f32[1,8,128]{2,1,0:T(8,128)}, u32[]{:S(2)}) copy-start(f32[1,8,128]{2,1,0:T(8,128)} %param.9) | copy-start | bytes 12292
  0.7 1.0 %copy-start = (f32[64,1024]{1,0:T(8,128)S(1)}, f32[64,1024]{1,0:T(8,128)}, u32[]{:S(2)}) copy-start(f32[64,1024]{1,0:T(8,128)} %ens_ref.1) | copy-start | bytes 786436
  1.7 0.9 %copy-start.1 = (f32[64,1024]{1,0:T(8,128)S(1)}, f32[64,1024]{1,0:T(8,128)}, u32[]{:S(2)}) copy-start(f32[64,1024]{1,0:T(8,128)} %obs_ref.1) | copy-start | bytes 786436

commit v6 on v5

--- a/solution.py
+++ b/solution.py
@@ -55,10 +55,11 @@
         return pl.ds(pl.multiple_of(which * rows, rows), rows)
 
     parts_in = obs_send.shape[1]
-    part = rows // parts_in
-
-    def part_of(which, at):
-        return pl.ds(pl.multiple_of(which * rows + at * part, part), part)
+    part = own_obs // parts_in
+    part_blocks = part // width
+
+    def part_of(slot, which, at):
+        return obs_all.at[slot, rows_of(which), pl.ds(at * part, part)]
 
     def points_of(which):
         return pl.ds(pl.multiple_of(which * points, points), points)
@@ -91,23 +92,23 @@
     def gather(step, at):
         if relay and step == 3:
             source, target = (2, 1) if at % 2 == 0 else (1, 2)
-            piece = part_of(flipped(me, source), at)
+            piece = part_of(1, flipped(me, source), at)
             return pltpu.make_async_remote_copy(
-                src_ref=obs_all.at[1, piece], dst_ref=obs_all.at[1, piece],
+                src_ref=piece, dst_ref=piece,
                 send_sem=obs_send.at[step, at], recv_sem=obs_recv.at[step, at],
                 device_id=(flipped(me, target), region), device_id_type=MESH,
             )
         return pltpu.make_async_remote_copy(
-            src_ref=obs_ref.at[pl.ds(at * part, part)], dst_ref=obs_all.at[1, part_of(me, at)],
+            src_ref=obs_ref.at[:, pl.ds(at * part, part)], dst_ref=part_of(1, me, at),
             send_sem=obs_send.at[step, at], recv_sem=obs_recv.at[step, at],
             device_id=(flipped(me, step), region), device_id_type=MESH,
         )
 
     def halo(step, at, other, side):
-        piece = part_of(flipped(me, step), at)
-        return pltpu.make_async_remote_copy(
-            src_ref=obs_ref.at[pl.ds(at * part, part)] if step == 0 else obs_all.at[1, piece],
-            dst_ref=obs_all.at[2 - 2 * side, piece],
+        owner = flipped(me, step)
+        return pltpu.make_async_remote_copy(
+            src_ref=obs_ref.at[:, pl.ds(at * part, part)] if step == 0 else part_of(1, owner, at),
+            dst_ref=part_of(2 - 2 * side, owner, at),
             send_sem=halo_send.at[side, step, at], recv_sem=halo_recv.at[side, step, at],
             device_id=(me, other), device_id_type=MESH,
         )
@@ -158,9 +159,11 @@
     for at in range(parts_in):
         for step in range(1, direct):
             pass_on(step, at)
-    for at in range(parts_in):
         for step in range(direct, n_mem):
-            pass_on(step, at)
+            if at > 0:
+                pass_on(step, at - 1)
+    for step in range(direct, n_mem):
+        pass_on(step, parts_in - 1)
 
     own_ens_copy.wait()
     for step in range(1, n_mem):
@@ -170,18 +173,19 @@
     anomalies = ensemble - mean
     anomaly_halves = halves(anomalies)
 
-    def add_region(slot):
-        first = (region - 1 + slot) * own_blocks
+    def add_part(slot, piece):
+        first = (region - 1 + slot) * own_blocks + piece * part_blocks
         parts = []
-        for at in range(own_blocks):
+        for at in range(part_blocks):
             chosen = jnp.where(block_ref[...] == first + at, weight_ref[...], 0.0)
             parts.append(jnp.sum(chosen, axis=0, keepdims=True))
-        block = obs_all[slot]
+        columns_here = slice(piece * part, (piece + 1) * part)
+        block = obs_all[slot, :, columns_here]
         scaled = block * jnp.concatenate(parts, axis=1)
         gram[...] += product(halves(scaled), halves(block), NT)
-        driven = scaled * innov_all[slot]
+        driven = scaled * innov_all[slot, :, columns_here]
         total = driven[:, :width]
-        for at in range(1, own_blocks):
+        for at in range(1, part_blocks):
             total = total + driven[:, at * width : (at + 1) * width]
         drive_parts[...] += total
 
@@ -189,15 +193,19 @@
     drive_parts[...] = jnp.zeros_like(drive_parts)
     own_obs_copy.wait()
     own_innov_copy.wait()
-    add_region(1)
+    for at in range(parts_in):
+        add_part(1, at)
     for there, other, side in sides:
         @pl.when(there)
         def _():
-            for step in range(n_mem):
-                for at in range(parts_in):
+            innov(other, 1 - side).wait_recv()
+    for at in range(parts_in):
+        for there, other, side in sides:
+            @pl.when(there)
+            def _():
+                for step in range(n_mem):
                     halo(step, at, other, 1 - side).wait_recv()
-            innov(other, 1 - side).wait_recv()
-            add_region(2 * side)
+                add_part(2 * side, at)
 
     row_at = lax.broadcasted_iota(jnp.int32, (members, members), 0)
     column_at = lax.broadcasted_iota(jnp.int32, (members, members), 1)
@@ -255,7 +263,8 @@
     own_obs = obs_pert.shape[1]
     listed, width = loc_weights.shape[1:]
     members, points = rows * n_mem, own_points // n_mem
-    parts_in = 4 if rows % 32 == 0 else 2 if rows % 16 == 0 else 1
+    blocks = own_obs // width
+    parts_in = 4 if blocks % 4 == 0 else 2 if blocks % 2 == 0 else 1
     return pl.pallas_call(
         functools.partial(kernel, n_mem, n_reg),
         out_shape=jax.ShapeDtypeStruct((rows, own_points), jnp.float32),

time: 35.1 us -> 37.2 us (1.060)
  Pallas kernels: 31.6 us -> 33.6 us
    pallas_call x1, Pallas kernels: 31.6 us -> 33.6 us  [on_device(): pl.pallas_call(functools.partial(kernel, n_mem, n_reg), out_shape=jax.Sha...]
where the time goes in v6:
time: 37.2 us; the launch traced here: 37 us
  Pallas kernels  33.6 us (90%)
  local copies, waits for them, and re-layouts  3.34 us (9%)
    pallas_call x1, Pallas kernels, on_device(): pl.pallas_call(functools.partial(kernel, n_mem, n_reg), out_shape=jax.Sha...  33.6 us
    unnamed x11, local copies, waits for them, and re-layouts  3.26 us

profile of v6, /device:TPU:1, one launch (start us, length us, event | category | flops | bytes accessed | tf_op | source)
XLA Modules:
  0.0 37.0 jit_solution(9015551409584080858)
XLA Ops:
  0.0 0.0 copy-start.4
  0.0 0.0 copy-start.2
  0.0 0.0 copy-start.3
  0.0 0.6 %copy-done.4 = s32[1,8]{1,0:T(1,128)S(1)} copy-done((s32[1,8]{1,0:T(1,128)S(1)}, s32[1,8]{1,0:T(1,128)}, u32[]{:S(2)}) %copy-start.4) | copy-done | bytes 56
  0.7 0.1 copy.6.block_ref
  0.7 0.0 copy-done.2
  0.7 0.0 copy-done.3
  0.7 0.0 copy-start
  0.7 0.9 %copy-done = f32[64,1024]{1,0:T(8,128)S(1)} copy-done((f32[64,1024]{1,0:T(8,128)S(1)}, f32[64,1024]{1,0:T(8,128)}, u32[]{:S(2)}) %copy-start) | copy-done | bytes 262168
  1.7 0.0 copy-start.1
  1.7 0.9 %copy-done.1 = f32[64,1024]{1,0:T(8,128)S(1)} copy-done((f32[64,1024]{1,0:T(8,128)S(1)}, f32[64,1024]{1,0:T(8,128)}, u32[]{:S(2)}) %copy-start.1) | copy-done | bytes 262168
  2.6 33.6 %shard_map.55 = f32[64,1024]{1,0:T(8,128)S(1)} custom-call(s32[8,1]{1,0:T(8,128)S(1)} %copy.6.block_ref, f32[64,1024]{1,0:T(8,128)S(1)} %copy-done, f32[64,1024]{1,0:T(8,128)S(1)} %copy-done.1, f32[1,1024]{1,0:T(1,128)S(1)} %bitcast.3, f32[8,128]{1,0:T(8,128)S(1)} %bitcast.4), custom_call_target="tpu_custom_call" | custom-call | tf_op jit(solution)/shard_map/pallas_call | solution.py:268
  36.3 0.7 %copy.8 = f32[64,1024]{1,0:T(8,128)} copy(f32[64,1024]{1,0:T(8,128)S(1)} %shard_map.55) | data formatting | bytes 524288
Async XLA Ops:
  0.0 0.7 %copy-start.4 = (s32[1,8]{1,0:T(1,128)S(1)}, s32[1,8]{1,0:T(1,128)}, u32[]{:S(2)}) copy-start(s32[1,8]{1,0:T(1,128)} %param.8) | copy-start | bytes 100
  0.0 0.7 %copy-start.2 = (f32[1024]{0:T(1024)S(1)}, f32[1024]{0:T(1024)}, u32[]{:S(2)}) copy-start(f32[1024]{0:T(1024)} %param.7) | copy-start | bytes 12292
  0.0 0.7 %copy-start.3 = (f32[1,8,128]{2,1,0:T(8,128)S(1)}, f32[1,8,128]{2,1,0:T(8,128)}, u32[]{:S(2)}) copy-start(f32[1,8,128]{2,1,0:T(8,128)} %param.9) | copy-start | bytes 12292
  0.7 1.0 %copy-start = (f32[64,1024]{1,0:T(8,128)S(1)}, f32[64,1024]{1,0:T(8,128)}, u32[]{:S(2)}) copy-start(f32[64,1024]{1,0:T(8,128)} %ens_ref.1) | copy-start | bytes 786436
  1.7 0.9 %copy-start.1 = (f32[64,1024]{1,0:T(8,128)S(1)}, f32[64,1024]{1,0:T(8,128)}, u32[]{:S(2)}) copy-start(f32[64,1024]{1,0:T(8,128)} %obs_ref.1) | copy-start | bytes 786436
